TPU v7x, 256 devices: a whole 4x4x8 slice. The times are simulated.
256 devices in a mesh: bx: 4 (over x), by: 4 (over y), vert: 16 (over z, core).
Axes of the slice: x: 4, y: 4, z: 8, core: 2. Of those that a mesh axis runs over, the one named last changes fastest.
Arguments:
- estimate: float32 [128, 128, 512], P('bx', 'by', 'vert'), may hold values from 0.5 to 1.5
- view_tiles: bfloat16 [4, 4, 16, 64, 64, 128], P('bx', 'by', 'vert'), may hold values from 0.19921875 to 2
- slot_view: int32 [4, 4, 4], P('bx', 'by'), may hold values from 0 to 3, each once within a row
- psf_taps: float32 [4, 3, 3, 33], replicated, may hold values from 0.05 to 1
Outputs:
- refined: float32 [128, 128, 512], P('bx', 'by', 'vert')
Inputs may be any that keep to these rules, and one draw needn't show every extreme that they name: `slot_view`: each block's list names every view once.
All inputs are finite; a program needn't handle non-finite values.
Results may differ from a plain program's by a relative error of at most 0.0003.
Values may be sent and summed in bfloat16 or wider, within the bound.
A program may use at most 128 MiB of HBM per device.

v0:
```python
import jax
import jax.numpy as jnp
from jax import lax
from jax.experimental import pallas as pl
from jax.experimental.pallas import tpu as pltpu
from jax.sharding import PartitionSpec as P

BACKGROUND = 0.1
MESH = pl.DeviceIdType.MESH
F32, BF16 = jnp.float32, jnp.bfloat16
BLOCK = 32
RAD = 16
TAPS = 33
RANK = 3
VIEWS = 4
GROUPS = 4
LANES = 128


def iota(shape, axis):
    return lax.broadcasted_iota(jnp.int32, shape, axis)


def dot(a, b):
    return jnp.dot(a, b, preferred_element_type=F32)


def band(line, rows, start):
    line = jnp.broadcast_to(line, (rows, LANES))
    return pltpu.roll(line, start % LANES, 1, stride=1, stride_axis=0)


def swap_quads(a, b):
    low, axis = iota(a.shape, a.ndim - 2) < 4, a.ndim - 2
    return jnp.where(low, a, pltpu.roll(b, 4, axis)), jnp.where(low, pltpu.roll(a, 4, axis), b)


def build_taps(psf, slot_view, slot, taps):
    listed = slot_view[...]
    view = jnp.sum(jnp.where(iota(listed.shape, 2) == slot, listed, 0), axis=2, keepdims=True)
    held = iota((VIEWS, TAPS), 0) == view[0]
    mine = jnp.sum(jnp.where(held[None, None], psf[...], 0.0), axis=2)
    mine = (mine / jnp.sum(mine, axis=-1, keepdims=True)).astype(BF16).astype(F32)
    taps[...] = jnp.zeros_like(taps)
    for a in range(3):
        taps[0, 8 * a : 8 * a + RANK, :TAPS] = mine[a]
    flip = (iota((LANES, LANES), 0) + iota((LANES, LANES), 1) == TAPS - 1).astype(BF16)
    taps[1] = dot(taps[0].astype(BF16), flip)


def build_z(taps, wz, wb):
    z_in, z_out = iota((LANES, LANES), 0), iota((LANES, LANES), 1)
    near = jnp.abs(z_in - z_out) <= RAD
    rim, out = iota((32, LANES), 0), iota((32, LANES), 1)
    rim_ok = ((rim < RAD) & (out <= rim)) | ((rim >= RAD) & (out >= rim + 96))
    lane16 = iota((16, LANES), 1)
    for r in range(RANK):
        forward, backward = taps[1, 16 + r : 17 + r, :], taps[0, 16 + r : 17 + r, :]
        columns = slice(r * LANES, (r + 1) * LANES)
        wz[0:128, columns] = jnp.where(near, band(forward, LANES, -RAD), 0.0).astype(BF16)
        wz[128:160, columns] = jnp.where(rim_ok, band(forward, 32, 96), 0.0).astype(BF16)
        wz[160:256, columns] = jnp.zeros((96, LANES), BF16)
        main = jnp.where(near, band(backward, LANES, -RAD), 0.0)
        low = jnp.where(lane16 < RAD, band(backward, 16, 0), 0.0)
        high = jnp.where(lane16 < RAD, band(backward, 16, 96), 0.0)
        for g in range(GROUPS):
            wb[g, r * 128 : r * 128 + 128, 0:128] = (
                pltpu.roll(main, 32 * g, 1) if g else main
            ).astype(BF16)
            wb[g, r * 128 : r * 128 + 128, 128:256] = jnp.zeros((128, LANES), BF16)
            lo, hi = pltpu.roll(low, RAD * g, 1) if g else low, pltpu.roll(high, 64 + RAD * g, 1)
            wb[g, r * 128 : r * 128 + 16, 128:256] = lo.astype(BF16)
            wb[g, r * 128 + 112 : r * 128 + 128, 128:256] = hi.astype(BF16)


def build_x(taps, bx, tx, txb):
    spread = (iota((LANES, 256), 1) == 4 * iota((LANES, 256), 0)).astype(BF16)
    lane, row = iota((LANES, LANES), 1), iota((LANES, LANES), 0)
    low, high = bx > 0, bx < 3

    def tiles(line):
        turned = [band(line[:, i * LANES : (i + 1) * LANES], LANES, 0) for i in range(2)]
        return jnp.where(lane >= row, turned[0], 0.0), jnp.where(lane >= row, turned[1], turned[0])

    wide = [dot(taps[k, 0:8, :].astype(BF16), spread) for k in range(2)]
    for r in range(RANK):
        left, right = tiles(wide[0][r : r + 1])
        tx[r, :, 0:128] = left.astype(BF16)
        tx[r, :, 128:256] = right.astype(BF16)
        left, right = [m[0:64] for m in tiles(wide[1][r : r + 1])]
        txb[0, r, :, 0:128] = jnp.where((lane[0:64] >= 64) | low, left, 0.0).astype(BF16)
        txb[0, r, :, 128:256] = right.astype(BF16)
        txb[1, r, :, 0:128] = left.astype(BF16)
        txb[1, r, :, 128:256] = jnp.where(high, right, 0.0).astype(BF16)


def build_y(taps, by, ty, tyb):
    place = by * BLOCK - RAD + iota((BLOCK, LANES), 1)
    inside = (place >= 0) & (place < 4 * BLOCK)
    plain = [band(taps[0, 8 + r : 9 + r, :], BLOCK, 0) for r in range(RANK)]
    plain += [
        jnp.where(inside, band(taps[1, 8 + r : 9 + r, :], BLOCK, 0), 0.0) for r in range(RANK)
    ]
    plain = jnp.concatenate(plain, axis=0).astype(BF16)
    y, column = iota((LANES, 256), 0), iota((LANES, 256), 1)
    wide = [
        dot(plain, (column == 16 * (y // 4) + 4 * x + y % 4).astype(BF16)).astype(BF16)
        for x in range(4)
    ]
    row, source = iota((LANES, LANES), 0), iota((LANES, LANES), 1)
    order = (row == 16 * (source % 32 // 4) + 4 * (source // 32) + source % 4).astype(BF16)
    for i in range(2 * RANK):
        done = dot(order, jnp.concatenate([m[i * 32 : i * 32 + 32] for m in wide], axis=0)).astype(BF16)
        if i < RANK:
            ty[i] = done
        else:
            tyb[(i - RANK) * 128 : (i - RANK + 1) * 128, :] = done


def kernel(
    est_hbm, tile_hbm, psf_hbm, slot_view_hbm, refined,
    est, tile, psf, slot_view,
    packed, parts, field, after_z, after_x, seen, back_y, back_x, sums, rims,
    got_core, got_rim, got_chip, got_edge,
    taps, tx, ty, wz, tyb, txb, wb,
    load_sem, part_send, part_recv, face_send, face_recv, core_send, core_recv, sum_send, sum_recv,
):
    bx, by, vert = lax.axis_index("bx"), lax.axis_index("by"), lax.axis_index("vert")
    q, slot = vert // VIEWS, vert % VIEWS
    core, chip = slot % 2, slot // 2

    loads = [
        pltpu.make_async_copy(source, target, load_sem.at[i])
        for i, (source, target) in enumerate(
            ((est_hbm, est), (psf_hbm, psf), (slot_view_hbm, slot_view), (tile_hbm, tile))
        )
    ]
    for copy in loads:
        copy.start()

    def at_vert(index):
        return {"vert": index}

    partner = at_vert(q * 4 + chip * 2 + 1 - core)
    x_up, x_down = ({"bx": bx + 1}, bx < 3), ({"bx": bx - 1}, bx > 0)
    y_up, y_down = ({"by": by + 1}, by < 3), ({"by": by - 1}, by > 0)
    above, below = q < 3, q > 0
    first, last = slot == 0, slot == VIEWS - 1
    is_edge = (first & below) | (last & above)

    def exists(jy, jx):
        here = jy == jy
        for index, j in ((by, jy), (bx, jx)):
            if j != 1:
                here = (index > 0 if j == 0 else index < 3) & here
        return here

    got_edge[...] = jnp.zeros_like(got_edge)
    barrier = pltpu.get_barrier_semaphore()

    def greet(device):
        pl.semaphore_signal(barrier, inc=1, device_id=device, device_id_type=MESH)

    for k in range(1, VIEWS):
        greet(at_vert(q * 4 + (slot + k) % VIEWS))
    for device, there in (x_up, x_down, y_up, y_down):
        pl.when(there)(lambda device=device: greet(device))

    @pl.when(below)
    def _():
        greet(at_vert(vert - slot - 1))
        pl.when(first)(lambda: greet(at_vert(vert - 3)))

    @pl.when(above)
    def _():
        greet(at_vert(vert - slot + 4))
        pl.when(last)(lambda: greet(at_vert(vert + 3)))

    loads[0].wait()
    groups = est[...].reshape(BLOCK, GROUPS, 8, BLOCK)
    line = jnp.concatenate([groups[:, g].reshape(256, BLOCK) for g in range(GROUPS)], axis=1)
    line = pltpu.roll(line, slot * 32, 1).reshape(16, 2, 8, LANES)
    for side, quads in enumerate(swap_quads(line[:, 0], line[:, 1])):
        packed[side * 128 : side * 128 + 128, :] = quads.reshape(128, LANES).astype(BF16)

    beside = [(there, 1) for _, there in (x_up, x_down, y_up, y_down)] + [(is_edge, 4)]
    beside += [((slot == 1) & above, 1), ((slot == 2) & below, 1)]
    pl.semaphore_wait(barrier, 3 + sum(jnp.where(there, n, 0) for there, n in beside))

    def part_copy(source, tp, send, device, side):
        return pltpu.make_async_remote_copy(
            src_ref=packed.at[pl.ds(side * 128 + tp * 64, 64), :], dst_ref=parts.at[source, tp],
            send_sem=part_send.at[send * 2 + tp], recv_sem=part_recv.at[source * 2 + tp],
            device_id=device, device_id_type=MESH,
        )

    for tp in range(2):
        for k in range(1, VIEWS):
            other = (slot + k) % VIEWS
            part_copy(slot, tp, k - 1, at_vert(q * 4 + other), other % 2).start()

        @pl.when(last & above)
        def _():
            for k in range(VIEWS):
                part_copy(4, tp, 3 + k, at_vert(vert + 1 + k), k % 2).start()

        @pl.when(first & below)
        def _():
            for k in range(VIEWS):
                part_copy(5, tp, 3 + k, at_vert(vert - 4 + k), k % 2).start()

    parts[slot] = packed[pl.ds(core * 128, 128), :].reshape(2, 64, LANES)

    def clear(ref):
        ref[...] = jnp.zeros(ref.shape, BF16)

    pl.when(~below)(lambda: clear(parts.at[4]))
    pl.when(~above)(lambda: clear(parts.at[5]))
    pl.when(bx == 0)(lambda: clear(field.at[:, :, :, 0:128, :]))
    pl.when(bx == 3)(lambda: clear(field.at[:, :, :, 256:384, :]))
    pl.when(by == 0)(lambda: clear(field.at[0]))
    pl.when(by == 3)(lambda: clear(field.at[2]))
    loads[1].wait()
    loads[2].wait()
    build_taps(psf, slot_view, slot, taps)
    build_z(taps, wz, wb)

    def assemble(tp):
        for k in range(1, VIEWS):
            part_copy((slot + k) % VIEWS, tp, 0, partner, 0).wait_recv()
        for k, there in ((4, below), (5, above)):
            pl.when(there)(lambda k=k: part_copy(k, tp, 0, partner, 0).wait_recv())
        lane = iota((64, LANES), 1)
        rows = slice(128 + tp * 64, 192 + tp * 64)
        have = [parts[k, tp].astype(F32) for k in range(6)]
        for g in range(GROUPS):
            line = have[(3 - g) % 4]
            for at in range(3):
                line = jnp.where(lane // 32 == at, have[(at - g) % 4], line)
            if g:
                line = pltpu.roll(line, LANES - 32 * g, 1)
            field[1, g, core, rows, :] = line.astype(BF16)
        line = pltpu.roll(jnp.where(lane % 32 < RAD, have[5], have[4]), RAD, 1)
        field[1, 4, core, rows, :] = line.astype(BF16)

    def piece(jy, jx, tp, side):
        return field.at[jy, :, side, pl.ds(jx * 128 + tp * 64, 64), :]

    def number(jy, jx, tp):
        return (jy * 3 + jx) * 2 + tp

    def face_copy(source, target, tp, send, device):
        return pltpu.make_async_remote_copy(
            src_ref=piece(*source, tp, core), dst_ref=piece(*target, tp, core),
            send_sem=face_send.at[send], recv_sem=face_recv.at[number(*target, tp)],
            device_id=device, device_id_type=MESH,
        )

    def core_copy(jy, jx, tp, side):
        return pltpu.make_async_remote_copy(
            src_ref=piece(jy, jx, tp, side), dst_ref=piece(jy, jx, tp, side),
            send_sem=core_send.at[number(jy, jx, tp)], recv_sem=core_recv.at[number(jy, jx, tp)],
            device_id=partner, device_id_type=MESH,
        )

    faces = []

    def send_face(source, target, tp, way):
        device, there = way
        copy = face_copy(source, target, tp, len(faces), device)
        there = there & exists(*source)
        pl.when(there)(copy.start)
        faces.append((copy, there))

    def arrived(jy, jx, tp):
        @pl.when(exists(jy, jx))
        def _():
            face_copy((jy, jx), (jy, jx), tp, 0, partner).wait_recv()
            core_copy(jy, jx, tp, core).start()

    def swapped(jy, jx):
        @pl.when(exists(jy, jx))
        def _():
            for tp in range(2):
                core_copy(jy, jx, tp, 1 - core).wait_recv()

    def forward_z(jy, jx):
        rows = slice(jx * 128, jx * 128 + 128)
        rim = field[jy, 4, :, rows, :].reshape(256, LANES)
        for g in range(GROUPS):
            turned = pltpu.roll(rim, LANES - 32 * g, 1) if g else rim
            main = field[jy, g, :, rows, :].reshape(256, LANES)
            done = dot(jnp.concatenate([main, turned], axis=1), wz[...]).astype(BF16)
            for r in range(RANK):
                after_z[r, jy * GROUPS + g, :, rows, :] = done[:, r * 128 : (r + 1) * 128].reshape(
                    2, 128, LANES
                )

    def forward_x(jy):
        def body(step, carry):
            r, group = step // GROUPS, jy * GROUPS + step % GROUPS
            for b in range(2):
                rows = pl.ds(b * 128, 256)
                both = jnp.concatenate([after_z[r, group, k, rows, :] for k in range(2)], axis=1)
                done = dot(tx[r], both).astype(BF16)
                for k in range(2):
                    after_x[r, group, k, b * 128 : b * 128 + 128, :] = done[:, k * 128 : k * 128 + 128]
            return carry

        lax.fori_loop(0, GROUPS * RANK, body, 0, unroll=True)

    for tp in (0, 1):
        assemble(tp)
        send_face((1, 1), (1, 0), tp, x_up)
        send_face((1, 1), (1, 2), tp, x_down)
        send_face((1, 1), (0, 1), tp, y_up)
        send_face((1, 1), (2, 1), tp, y_down)
        core_copy(1, 1, tp, core).start()
    build_x(taps, bx, tx, txb)
    for side in (0, 2):
        arrived(1, side, 0)
        send_face((1, side), (0, side), 0, y_up)
        send_face((1, side), (2, side), 0, y_down)
    for side in (0, 2):
        arrived(side, 1, 1)
        send_face((side, 1), (side, 0), 1, x_up)
        send_face((side, 1), (side, 2), 1, x_down)
    build_y(taps, by, ty, tyb)
    loads[3].wait()

    def order_tile(i, carry):
        quad = tile[pl.ds(4 * i, 4)].astype(F32).reshape(2, 2, 8, 8, LANES)
        sides = swap_quads(quad[:, 0], quad[:, 1])
        rows = jnp.stack([m[x] for m in sides for x in range(2)], axis=1)
        seen[i] = rows.reshape(256, LANES).astype(BF16)
        return carry

    lax.fori_loop(0, 16, order_tile, 0, unroll=4)
    swapped(1, 1)
    forward_z(1, 1)
    for side in (0, 2):
        arrived(1, side, 1)
        arrived(side, 1, 0)
    for side in (0, 2):
        swapped(1, side)
        swapped(side, 1)
    for side in (0, 2):
        forward_z(1, side)
        forward_z(side, 1)
    forward_x(1)
    for jy in (0, 2):
        for jx in (0, 2):
            for tp in range(2):
                arrived(jy, jx, tp)
    for jy in (0, 2):
        for jx in (0, 2):
            swapped(jy, jx)
    for jy in (0, 2):
        for jx in (0, 2):
            forward_z(jy, jx)
        forward_x(jy)

    def along_y(step):
        quotient = []
        for b in range(2):
            blurred = None
            for r in range(RANK):
                both = [
                    after_x[r, 4 * b : 4 * b + 8, :, pl.ds(32 * step + 16 * k, 16), :].reshape(256, LANES)
                    for k in range(2)
                ]
                part = dot(ty[r], jnp.concatenate(both, axis=1))
                blurred = part if blurred is None else blurred + part
            rows = slice(128 * b, 128 * b + 128)
            both = jnp.concatenate([seen[2 * step + k, rows, :] for k in range(2)], axis=1).astype(F32)
            quotient.append((RANK * both / (blurred + RANK * BACKGROUND)).astype(BF16))
        quotient = jnp.concatenate(quotient, axis=0)
        for r in range(RANK):
            done = dot(tyb[r * 128 : r * 128 + 128, :], quotient).astype(BF16)
            for k in range(2):
                back_y[r * 8 : r * 8 + 8, pl.ds(32 * step + 16 * k, 16), :] = done[
                    :, k * 128 : k * 128 + 128
                ].reshape(8, 16, LANES)

    def backward_x(half):
        within = slice(half * 64, half * 64 + 192)
        for g in range(GROUPS):
            for r in range(RANK):
                at = (r * GROUPS + g) * 2
                both = jnp.concatenate([back_y[at, within, :], back_y[at + 1, within, :]], axis=1)
                done = dot(txb[half, r, :, 0:192], both).astype(BF16)
                for k in range(2):
                    back_x[g, half, k * 64 : k * 64 + 64, r * 128 : (r + 1) * 128] = done[
                        :, k * 128 : k * 128 + 128
                    ]

    def backward_rims(half):
        both = dot(back_x[0, half], wb[0, :, LANES:])
        for g in range(1, GROUPS):
            both = both + dot(back_x[g, half], wb[g, :, LANES:])
        is_low = iota((64, LANES), 1) < 64
        rims[half, 0] = jnp.where(is_low, both[0:64], pltpu.roll(both[64:128], 64, 1))
        rims[half, 1] = jnp.where(is_low, pltpu.roll(both[0:64], 64, 1), both[64:128])

    def backward_z(half):
        for g in range(GROUPS):
            done = dot(back_x[g, half], wb[g, :, :LANES])
            for c in range(4):
                at = (g + c) % 4
                sums[half, c, :, at * 32 : at * 32 + 32] = done[:, at * 32 : at * 32 + 32]

    far = (1 - chip) * 2 + core

    def sum_copy(source, target, index, device):
        return pltpu.make_async_remote_copy(
            src_ref=source, dst_ref=target, send_sem=sum_send.at[index],
            recv_sem=sum_recv.at[index], device_id=device, device_id_type=MESH,
        )

    far_swap = [
        sum_copy(sums.at[h, (1 - chip) * 2 + 1 - core], got_core.at[h, 0], h, partner) for h in range(2)
    ]
    near_swap = [
        sum_copy(sums.at[h, chip * 2 + 1 - core], got_core.at[h, 1], 2 + h, partner) for h in range(2)
    ]
    over = [sum_copy(sums.at[h, far], got_chip.at[h], 4 + h, at_vert(q * 4 + far)) for h in range(2)]
    rim_swap = [sum_copy(rims.at[h, 1 - core], got_rim.at[h], 6 + h, partner) for h in range(2)]
    edge_home = jnp.where(core == 0, vert - slot - 1, vert - slot + 4)
    edge_there = jnp.where(core == 0, q, 3 - q) > 0

    def edge_copy(h, which):
        return pltpu.make_async_remote_copy(
            src_ref=rims.at[h, core], dst_ref=got_edge.at[which, h], send_sem=sum_send.at[8 + h],
            recv_sem=sum_recv.at[8 + 2 * h + which], device_id=at_vert(edge_home), device_id_type=MESH,
        )

    def backward(h):
        backward_x(h)
        backward_rims(h)
        rim_swap[h].start()
        backward_z(h)
        far_swap[h].start()
        near_swap[h].start()

    def pass_over(h):
        rim_swap[h].wait_recv()
        rims[h, core] = rims[h, core] + got_rim[h]
        pl.when(edge_there)(lambda: edge_copy(h, chip).start())
        far_swap[h].wait_recv()
        sums[h, far] = sums[h, far] + got_core[h, 0]
        over[h].start()

    for step in range(6):
        along_y(step)
    backward(0)
    for step in range(6, 8):
        along_y(step)
    pass_over(0)
    backward(1)
    pass_over(1)

    mine = []
    for h in range(2):
        near_swap[h].wait_recv()
        mine.append(sums[h, slot] + got_core[h, 1])
    for h in range(2):
        over[h].wait_recv()
        mine[h] = mine[h] + got_chip[h]

    @pl.when(is_edge)
    def _():
        for h in range(2):
            edge_copy(h, 0).wait_recv()
            edge_copy(h, 1).wait_recv()

    start = jnp.where(last, RAD, 0)
    lane = iota((64, LANES), 1)
    keep = is_edge & (lane >= start) & (lane < start + RAD)
    for h in range(2):
        edge = got_edge[0, h] + got_edge[1, h]
        for g in range(GROUPS):
            own = pltpu.roll(mine[h], (8 - g - slot) % 4 * 32, 1)
            sides = []
            for k in range(2):
                rim = pltpu.roll(edge, (start + LANES - 64 * k - RAD * g) % LANES, 1)
                part = own[64 * k : 64 * k + 64] + jnp.where(keep, rim, 0.0)
                sides.append(part.reshape(8, 8, LANES) * (1.0 / (RANK * VIEWS)))
            part = jnp.stack(swap_quads(*sides), axis=1).reshape(16, 8, LANES)
            at = (slice(16 * h, 16 * h + 16), slice(g * 8, g * 8 + 8))
            refined[at] = est[at] * part[:, :, 0:BLOCK]

    for tp in range(2):
        for k in range(1, VIEWS):
            part_copy(slot, tp, k - 1, partner, 0).wait_send()

        @pl.when(is_edge)
        def _():
            for k in range(VIEWS):
                part_copy(4, tp, 3 + k, partner, 0).wait_send()

    for copy, there in faces:
        pl.when(there)(copy.wait_send)
    for jy in range(3):
        for jx in range(3):

            @pl.when(exists(jy, jx))
            def _():
                for tp in range(2):
                    core_copy(jy, jx, tp, core).wait_send()

    for copy in far_swap + near_swap + over + rim_swap:
        copy.wait_send()

    @pl.when(edge_there)
    def _():
        for h in range(2):
            edge_copy(h, 0).wait_send()


def local(estimate, view_tiles, slot_view, psf_taps):
    vmem = pl.BlockSpec(memory_space=pltpu.VMEM)
    hbm = pl.BlockSpec(memory_space=pltpu.HBM)
    tile = view_tiles[0, 0, 0]
    psf = jnp.transpose(psf_taps, (1, 2, 0, 3))
    scratch = [
        pltpu.VMEM(estimate.shape, F32),
        pltpu.VMEM(tile.shape, BF16),
        pltpu.VMEM(psf.shape, F32),
        pltpu.VMEM(slot_view.shape, jnp.int32),
        pltpu.VMEM((256, LANES), BF16),
        pltpu.VMEM((6, 2, 64, LANES), BF16),
        pltpu.VMEM((3, 5, 2, 384, LANES), BF16),
        pltpu.VMEM((RANK, 12, 2, 384, LANES), BF16),
        pltpu.VMEM((RANK, 12, 2, 256, LANES), BF16),
        pltpu.VMEM((16, 256, LANES), BF16),
        pltpu.VMEM((24, 256, LANES), BF16),
        pltpu.VMEM((GROUPS, 2, 128, RANK * LANES), BF16),
        pltpu.VMEM((2, 4, 128, LANES), F32),
        pltpu.VMEM((2, 2, 64, LANES), F32),
        pltpu.VMEM((2, 2, 128, LANES), F32),
        pltpu.VMEM((2, 64, LANES), F32),
        pltpu.VMEM((2, 128, LANES), F32),
        pltpu.VMEM((2, 2, 64, LANES), F32),
        pltpu.VMEM((2, 24, LANES), F32),
        pltpu.VMEM((RANK, 128, 256), BF16),
        pltpu.VMEM((RANK, 128, 256), BF16),
        pltpu.VMEM((256, RANK * LANES), BF16),
        pltpu.VMEM((RANK * 128, 256), BF16),
        pltpu.VMEM((2, RANK, 64, 256), BF16),
        pltpu.VMEM((GROUPS, RANK * LANES, 256), BF16),
        pltpu.SemaphoreType.DMA((4,)),
        pltpu.SemaphoreType.DMA((14,)),
        pltpu.SemaphoreType.DMA((12,)),
        pltpu.SemaphoreType.DMA((16,)),
        pltpu.SemaphoreType.DMA((18,)),
        pltpu.SemaphoreType.DMA((18,)),
        pltpu.SemaphoreType.DMA((18,)),
        pltpu.SemaphoreType.DMA((10,)),
        pltpu.SemaphoreType.DMA((12,)),
    ]
    return pl.pallas_call(
        kernel,
        out_shape=pltpu.VMEM(estimate.shape, F32),
        in_specs=[hbm] * 4,
        out_specs=vmem,
        scratch_shapes=scratch,
        compiler_params=pltpu.CompilerParams(
            collective_id=0, has_side_effects=True, vmem_limit_bytes=56 * 1024 * 1024
        ),
    )(*(pltpu.with_memory_space_constraint(a, pltpu.HBM) for a in (estimate, tile, psf, slot_view)))


def solution(mesh):
    placed = (
        P("bx", "by", "vert"),
        P("bx", "by", "vert", None, None, None),
        P("bx", "by", None),
        P(),
    )
    return jax.shard_map(
        local, mesh=mesh, in_specs=placed, out_specs=P("bx", "by", "vert"), check_vma=False
    )
```

profile of v0, /device:TPU:43, one launch (start us, length us, event | category | flops | bytes accessed | tf_op | source)
XLA Modules:
  0.0 34.7 jit_solution(17907621108021491508)
XLA Ops:
  0.0 33.9 %shard_map.46 = f32[32,32,32]{2,1,0:T(8,128)S(1)} custom-call(f32[32,32,32]{2,1,0:T(8,128)} %est_hbm.1, bf16[64,64,128]{2,1,0:T(8,128)(2,1)} %bitcast.2, f32[3,3,4,33]{3,2,1,0:T(4,128)} %bitcast.3, s32[1,1,4]{2,1,0:T(1,128)} %slot_view_hbm.1), custom_call_target="tpu_custom_call" | custom-call | tf_op jit(solution)/shard_map/pallas_call | solution.py:561
  33.9 0.8 %copy.6 = f32[32,32,32]{2,1,0:T(8,128)} copy(f32[32,32,32]{2,1,0:T(8,128)S(1)} %shard_map.46) | data formatting | bytes 262144
where the time goes:
time: 34.8 us; the launch traced here: 34.7 us
  Pallas kernels  33.9 us (97%)
  local copies, waits for them, and re-layouts  0.8 us (2%)
    pallas_call x1, Pallas kernels, local(): pl.pallas_call(kernel, out_shape=pltpu.VMEM(estimate.shape, F32), in_spec...  33.9 us
    unnamed x1, local copies, waits for them, and re-layouts  0.8 us

commit v1 on v0

--- a/solution.py
+++ b/solution.py
@@ -309,22 +309,31 @@
 
         lax.fori_loop(0, GROUPS * RANK, body, 0, unroll=True)
 
-    for tp in (0, 1):
-        assemble(tp)
-        send_face((1, 1), (1, 0), tp, x_up)
-        send_face((1, 1), (1, 2), tp, x_down)
-        send_face((1, 1), (0, 1), tp, y_up)
-        send_face((1, 1), (2, 1), tp, y_down)
-        core_copy(1, 1, tp, core).start()
+    def send_faces(tp, ways):
+        for target, way in ways:
+            send_face((1, 1), target, tp, way)
+
+    along_x_links = (((1, 0), x_up), ((1, 2), x_down))
+    along_y_links = (((0, 1), y_up), ((2, 1), y_down))
+    assemble(0)
+    send_faces(0, along_x_links)
+    core_copy(1, 1, 0, core).start()
+    assemble(1)
+    send_faces(1, along_y_links)
+    send_faces(1, along_x_links)
+    send_faces(0, along_y_links)
+    core_copy(1, 1, 1, core).start()
     build_x(taps, bx, tx, txb)
     for side in (0, 2):
         arrived(1, side, 0)
-        send_face((1, side), (0, side), 0, y_up)
-        send_face((1, side), (2, side), 0, y_down)
+    for one, other in ((0, 2), (2, 0)):
+        send_face((1, one), (0, one), 0, y_up)
+        send_face((1, other), (2, other), 0, y_down)
     for side in (0, 2):
         arrived(side, 1, 1)
-        send_face((side, 1), (side, 0), 1, x_up)
-        send_face((side, 1), (side, 2), 1, x_down)
+    for one, other in ((0, 2), (2, 0)):
+        send_face((one, 1), (one, 0), 1, x_up)
+        send_face((other, 1), (other, 2), 1, x_down)
     build_y(taps, by, ty, tyb)
     loads[3].wait()
 
@@ -347,17 +356,20 @@
     for side in (0, 2):
         forward_z(1, side)
         forward_z(side, 1)
+    waves = (((0, 0), (2, 2)), ((0, 2), (2, 0)))
+    for corner in waves[0]:
+        for tp in range(2):
+            arrived(*corner, tp)
     forward_x(1)
+    for corner in waves[1]:
+        for tp in range(2):
+            arrived(*corner, tp)
+    for wave in waves:
+        for corner in wave:
+            swapped(*corner)
+        for corner in wave:
+            forward_z(*corner)
     for jy in (0, 2):
-        for jx in (0, 2):
-            for tp in range(2):
-                arrived(jy, jx, tp)
-    for jy in (0, 2):
-        for jx in (0, 2):
-            swapped(jy, jx)
-    for jy in (0, 2):
-        for jx in (0, 2):
-            forward_z(jy, jx)
         forward_x(jy)
 
     def along_y(step):

time: 34.8 us -> 33.2 us (0.954)
  Pallas kernels: 33.9 us -> 32.3 us
    pallas_call x1, Pallas kernels: 33.9 us -> 32.3 us  [local(): pl.pallas_call(kernel, out_shape=pltpu.VMEM(estimate.shape, F32), in_spec...]
where the time goes in v1:
time: 33.2 us; the launch traced here: 33.1 us
  Pallas kernels  32.3 us (97%)
  local copies, waits for them, and re-layouts  0.8 us (2%)
    pallas_call x1, Pallas kernels, local(): pl.pallas_call(kernel, out_shape=pltpu.VMEM(estimate.shape, F32), in_spec...  32.3 us
    unnamed x1, local copies, waits for them, and re-layouts  0.8 us

profile of v1, /device:TPU:43, one launch (start us, length us, event | category | flops | bytes accessed | tf_op | source)
XLA Modules:
  0.0 33.1 jit_solution(2534765287731255169)
XLA Ops:
  0.0 32.3 %shard_map.46 = f32[32,32,32]{2,1,0:T(8,128)S(1)} custom-call(f32[32,32,32]{2,1,0:T(8,128)} %est_hbm.1, bf16[64,64,128]{2,1,0:T(8,128)(2,1)} %bitcast.2, f32[3,3,4,33]{3,2,1,0:T(4,128)} %bitcast.3, s32[1,1,4]{2,1,0:T(1,128)} %slot_view_hbm.1), custom_call_target="tpu_custom_call" | custom-call | tf_op jit(solution)/shard_map/pallas_call | solution.py:573
  32.3 0.8 %copy.6 = f32[32,32,32]{2,1,0:T(8,128)} copy(f32[32,32,32]{2,1,0:T(8,128)S(1)} %shard_map.46) | data formatting | bytes 262144
